TPU v7x, 32 devices: a whole 2x2x4 slice. The times are simulated.
32 devices in a mesh: fsdp: 4 (over x, core), dp: 8 (over z, y).
Axes of the slice: x: 2, y: 2, z: 4, core: 2. Of those that a mesh axis runs over, the one named last changes fastest.
Arguments:
- tokens: bfloat16 [16384, 768], P(('fsdp', 'dp')), may hold values from -6 to 6
- cotangent: bfloat16 [16384, 768], P(('fsdp', 'dp')), may hold values from -6 to 6
- seq_lengths: int32 [32, 2], P(('fsdp', 'dp')), may hold values from 0 to 512, as said below
- routes: int32 [16384, 1], P(('fsdp', 'dp')), may hold values from 0 to 7; in each aligned block of 512 rows (0 to 511, 512 to 1023, ...) at most 128 rows name the same one
- bucket_table: int32 [1024], replicated, may hold values from 0 to 31, as said below
- w_query: bfloat16 [768, 768], P('fsdp'), may hold values from -0.109375 to 0.109375
- w_key: bfloat16 [768, 768], P('fsdp'), may hold values from -0.109375 to 0.109375
- w_value: bfloat16 [768, 768], P('fsdp'), may hold values from -0.21875 to 0.21875
- w_output: bfloat16 [768, 768], P('fsdp'), may hold values from -0.875 to 0.875
- w_router: bfloat16 [768, 8], P('fsdp'), may hold values from -0.15625 to 0.15625
- norm_attn: bfloat16 [768], P('fsdp'), may hold values from 0.5 to 1.5
- norm_ffn: bfloat16 [768], P('fsdp'), may hold values from 0.5 to 1.5
- rel_bias: bfloat16 [32, 12], P('fsdp'), may hold values from -4 to 4
- expert_in: bfloat16 [8, 768, 3072], P('dp', None, 'fsdp'), may hold values from -0.21875 to 0.21875
- expert_out: bfloat16 [8, 3072, 768], P('dp', 'fsdp'), may hold values from -0.875 to 0.875
Outputs:
- layer_out: bfloat16 [16384, 768], P(('fsdp', 'dp'))
- grad_tokens: bfloat16 [16384, 768], P(('fsdp', 'dp'))
- grad_query: float32 [768, 768], P('fsdp')
- grad_key: float32 [768, 768], P('fsdp')
- grad_value: float32 [768, 768], P('fsdp')
- grad_output: float32 [768, 768], P('fsdp')
- grad_router: float32 [768, 8], P('fsdp')
- grad_norm_attn: float32 [768], P('fsdp')
- grad_norm_ffn: float32 [768], P('fsdp')
- grad_rel_bias: float32 [32, 12], P('fsdp')
- grad_expert_in: float32 [8, 768, 3072], P('dp', None, 'fsdp')
- grad_expert_out: float32 [8, 3072, 768], P('dp', 'fsdp')
Inputs may be any that keep to these rules, and one draw needn't show every extreme that they name: `seq_lengths`: each row's lengths sum to 256 or more and at most 512; some row holds one sequence of 512. `routes`: no expert is named more than 128 times among the rows of one device, and in every draw some device names one expert exactly 128 times. `bucket_table`: entry 512 + j holds the bucket of offset j (key place minus query place); entry 0 is not read.
All inputs are finite; a program needn't handle non-finite values.
Results may differ from a plain program's by a relative error of at most 0.018.
Values may be sent and summed in bfloat16 or wider, within the bound.
A program may use at most 192 MiB of HBM per device.

v0:
```python
import jax
import jax.numpy as jnp
from jax import lax
from jax.sharding import PartitionSpec as P

D = 768
HEADS = 12
HEAD_DIM = 64


EPSILON = 1e-06
PRECISE = lax.Precision.HIGHEST
MASKED = -1e30


def norm_parts(values, gain_vec):
    scale_row = lax.rsqrt(jnp.mean(values * values, axis=-1, keepdims=True) + EPSILON)
    unit_rows = values * scale_row
    return (unit_rows * gain_vec, unit_rows, scale_row)


def norm_back(grad_rows, unit_rows, scale_row, gain_vec):
    gain_grad = jnp.sum(grad_rows * unit_rows, axis=0)
    scaled = grad_rows * gain_vec
    return (
        scale_row * (scaled - unit_rows * jnp.mean(scaled * unit_rows, axis=-1, keepdims=True)),
        gain_grad,
    )


def relative_bias(rel_table, bucket_table, tok_rows):
    buckets = rel_table.shape[0]
    bucket_hot = (bucket_table[:, None] == jnp.arange(buckets, dtype=jnp.int32)[None, :]).astype(
        jnp.float32
    )
    per_offset = jnp.dot(bucket_hot, rel_table, precision=PRECISE)
    rolled = jnp.roll(per_offset, -tok_rows, axis=0)
    per_head = jnp.transpose(rolled)
    heads_n = per_head.shape[0]
    span = 2 * tok_rows - 1
    flat = jnp.tile(per_head, (1, tok_rows))[:, : tok_rows * span]
    return flat.reshape(heads_n, tok_rows, span)[:, :, :tok_rows]


def masked_scores(query_heads, key_heads, pos_bias, same_seq):
    scores = (
        jnp.einsum("qhd,khd->hqk", query_heads, key_heads, preferred_element_type=jnp.float32)
        + pos_bias
    )
    return jnp.where(same_seq[None], scores, MASKED)


def gelu_grad(hidden_pre, grad_act):
    unused, pull_back = jax.vjp(jax.nn.gelu, hidden_pre)
    return pull_back(grad_act)[0]


def local(
    tokens,
    cotangent,
    seq_lengths,
    routes,
    bucket_table,
    w_query,
    w_key,
    w_value,
    w_output,
    w_router,
    norm_attn,
    norm_ffn,
    rel_bias,
    expert_in,
    expert_out,
):
    tok_rows = tokens.shape[0]
    experts = lax.axis_size("dp")
    capacity = 2 * tok_rows // experts
    width_all = HEADS * HEAD_DIM
    head_shape = (tok_rows, HEADS, HEAD_DIM)
    query_w, key_w, value_w, output_w, router_w, gain_attn, gain_ffn, rel_table = (
        lax.all_gather(w_query, "fsdp", axis=0, tiled=True),
        lax.all_gather(w_key, "fsdp", axis=0, tiled=True),
        lax.all_gather(w_value, "fsdp", axis=0, tiled=True),
        lax.all_gather(w_output, "fsdp", axis=0, tiled=True),
        lax.all_gather(w_router, "fsdp", axis=0, tiled=True),
        lax.all_gather(norm_attn, "fsdp", axis=0, tiled=True),
        lax.all_gather(norm_ffn, "fsdp", axis=0, tiled=True),
        lax.all_gather(rel_bias, "fsdp", axis=0, tiled=True),
    )
    gain_attn = gain_attn.astype(jnp.float32)
    gain_ffn = gain_ffn.astype(jnp.float32)
    rel_float = rel_table.astype(jnp.float32)
    position = jnp.arange(tok_rows, dtype=jnp.int32)
    ends_at = jnp.cumsum(seq_lengths[0])
    segment = jnp.sum((position[:, None] >= ends_at[None, :]).astype(jnp.int32), axis=1)
    same_seq = segment[:, None] == segment[None, :]
    inputs_f = tokens.astype(jnp.float32)
    normed_f, unit_one, scale_one = norm_parts(inputs_f, gain_attn)
    normed = normed_f.astype(jnp.bfloat16)
    query_heads = (
        jnp.dot(normed, query_w, preferred_element_type=jnp.float32)
        .astype(jnp.bfloat16)
        .reshape(head_shape)
    )
    key_heads = (
        jnp.dot(normed, key_w, preferred_element_type=jnp.float32)
        .astype(jnp.bfloat16)
        .reshape(head_shape)
    )
    value_heads = (
        jnp.dot(normed, value_w, preferred_element_type=jnp.float32)
        .astype(jnp.bfloat16)
        .reshape(head_shape)
    )
    pos_bias, bias_back = jax.vjp(
        lambda table_vals: relative_bias(table_vals, bucket_table, tok_rows), rel_float
    )
    scores = masked_scores(query_heads, key_heads, pos_bias, same_seq)
    row_max = jnp.max(scores, axis=-1, keepdims=True)
    log_total = row_max + jnp.log(jnp.sum(jnp.exp(scores - row_max), axis=-1, keepdims=True))
    attn_low = jnp.exp(scores - log_total).astype(jnp.bfloat16)
    attended = (
        jnp.einsum("hqk,khd->qhd", attn_low, value_heads, preferred_element_type=jnp.float32)
        .astype(jnp.bfloat16)
        .reshape(tok_rows, width_all)
    )
    residual = inputs_f + jnp.dot(attended, output_w, preferred_element_type=jnp.float32)
    ffn_f, unit_two, scale_two = norm_parts(residual, gain_ffn)
    ffn_in = ffn_f.astype(jnp.bfloat16)
    router_p = jax.nn.softmax(
        jnp.dot(ffn_in, router_w, preferred_element_type=jnp.float32), axis=-1
    )
    route_ids = routes[:, 0]
    hot_int = (route_ids[:, None] == jnp.arange(experts, dtype=jnp.int32)[None, :]).astype(
        jnp.int32
    )
    chosen = hot_int.astype(jnp.float32)
    gate_value = jnp.sum(router_p * chosen, axis=-1, keepdims=True)
    lower_tri = (position[:, None] > position[None, :]).astype(jnp.bfloat16)
    earlier = jnp.dot(lower_tri, chosen.astype(jnp.bfloat16), preferred_element_type=jnp.float32)
    slot_rank = jnp.sum(earlier * chosen, axis=1).astype(jnp.int32)
    slot_index = route_ids * capacity + slot_rank
    slot_ids = jnp.arange(experts * capacity, dtype=jnp.int32)
    slot_hot = (slot_ids[:, None] == slot_index[None, :]).astype(jnp.bfloat16)
    send_rows = jnp.dot(slot_hot, ffn_in, preferred_element_type=jnp.float32).astype(jnp.bfloat16)
    arrived = lax.all_to_all(
        send_rows.reshape(experts, capacity, D), "dp", split_axis=0, concat_axis=0, tiled=True
    ).reshape(experts * capacity, D)
    first_full, second_full = (
        lax.all_gather(expert_in, "fsdp", axis=2, tiled=True),
        lax.all_gather(expert_out, "fsdp", axis=1, tiled=True),
    )
    first_w = first_full[0]
    second_w = second_full[0]
    hidden_pre = jnp.dot(arrived, first_w, preferred_element_type=jnp.float32)
    hidden_act = jax.nn.gelu(hidden_pre).astype(jnp.bfloat16)
    expert_result = jnp.dot(hidden_act, second_w, preferred_element_type=jnp.float32).astype(
        jnp.bfloat16
    )
    returned = lax.all_to_all(
        expert_result.reshape(experts, capacity, D), "dp", split_axis=0, concat_axis=0, tiled=True
    ).reshape(experts * capacity, D)
    token_out = jnp.dot(slot_hot.T, returned, preferred_element_type=jnp.float32)
    layer_out = (residual + gate_value * token_out).astype(jnp.bfloat16)
    grad_out = cotangent.astype(jnp.float32)
    grad_gate = jnp.sum(grad_out * token_out, axis=-1, keepdims=True)
    grad_token_out = (gate_value * grad_out).astype(jnp.bfloat16)
    send_grads = jnp.dot(slot_hot, grad_token_out, preferred_element_type=jnp.float32).astype(
        jnp.bfloat16
    )
    grad_arrived = lax.all_to_all(
        send_grads.reshape(experts, capacity, D), "dp", split_axis=0, concat_axis=0, tiled=True
    ).reshape(experts * capacity, D)
    grad_act = jnp.dot(grad_arrived, second_w.T, preferred_element_type=jnp.float32)
    grad_pre = gelu_grad(hidden_pre, grad_act).astype(jnp.bfloat16)
    grad_expert_rows = jnp.dot(grad_pre, first_w.T, preferred_element_type=jnp.float32).astype(
        jnp.bfloat16
    )
    first_term = jnp.dot(arrived.T, grad_pre, preferred_element_type=jnp.float32)[None]
    second_term = jnp.dot(hidden_act.T, grad_arrived, preferred_element_type=jnp.float32)[None]
    grad_first, grad_second = (
        lax.psum_scatter(
            first_term.astype(jnp.bfloat16), "fsdp", scatter_dimension=2, tiled=True
        ).astype(jnp.float32),
        lax.psum_scatter(
            second_term.astype(jnp.bfloat16), "fsdp", scatter_dimension=1, tiled=True
        ).astype(jnp.float32),
    )
    grad_back = lax.all_to_all(
        grad_expert_rows.reshape(experts, capacity, D),
        "dp",
        split_axis=0,
        concat_axis=0,
        tiled=True,
    ).reshape(experts * capacity, D)
    grad_logits = router_p * (chosen - gate_value) * grad_gate
    ffn_float = ffn_in.astype(jnp.float32)
    grad_router_w = jnp.dot(ffn_float.T, grad_logits, precision=PRECISE)
    grad_ffn_in = jnp.dot(slot_hot.T, grad_back, preferred_element_type=jnp.float32) + jnp.dot(
        grad_logits, router_w.astype(jnp.float32).T, precision=PRECISE
    )
    grad_from_ffn, grad_gain_ffn = norm_back(grad_ffn_in, unit_two, scale_two, gain_ffn)
    grad_residual = grad_out + grad_from_ffn
    grad_att = grad_residual.astype(jnp.bfloat16)
    grad_output_w = jnp.dot(attended.T, grad_att, preferred_element_type=jnp.float32)
    grad_attended = (
        jnp.dot(grad_att, output_w.T, preferred_element_type=jnp.float32)
        .astype(jnp.bfloat16)
        .reshape(head_shape)
    )
    scores_again = masked_scores(query_heads, key_heads, pos_bias, same_seq)
    attn_float = jnp.exp(scores_again - log_total)
    grad_attn = jnp.einsum(
        "qhd,khd->hqk", grad_attended, value_heads, preferred_element_type=jnp.float32
    )
    grad_scores = (
        attn_float * (grad_attn - jnp.sum(attn_float * grad_attn, axis=-1, keepdims=True))
    ).astype(jnp.bfloat16)
    grad_v = (
        jnp.einsum(
            "hqk,qhd->khd",
            attn_float.astype(jnp.bfloat16),
            grad_attended,
            preferred_element_type=jnp.float32,
        )
        .astype(jnp.bfloat16)
        .reshape(tok_rows, width_all)
    )
    grad_q = (
        jnp.einsum("hqk,khd->qhd", grad_scores, key_heads, preferred_element_type=jnp.float32)
        .astype(jnp.bfloat16)
        .reshape(tok_rows, width_all)
    )
    grad_k = (
        jnp.einsum("hqk,qhd->khd", grad_scores, query_heads, preferred_element_type=jnp.float32)
        .astype(jnp.bfloat16)
        .reshape(tok_rows, width_all)
    )
    grad_rel = bias_back(grad_scores.astype(jnp.float32))[0]
    grad_query_w = jnp.dot(normed.T, grad_q, preferred_element_type=jnp.float32)
    grad_key_w = jnp.dot(normed.T, grad_k, preferred_element_type=jnp.float32)
    grad_value_w = jnp.dot(normed.T, grad_v, preferred_element_type=jnp.float32)
    grad_normed = jnp.dot(grad_q, query_w.T, preferred_element_type=jnp.float32)
    grad_normed = grad_normed + jnp.dot(grad_k, key_w.T, preferred_element_type=jnp.float32)
    grad_normed = grad_normed + jnp.dot(grad_v, value_w.T, preferred_element_type=jnp.float32)
    grad_from_attn, grad_gain_attn = norm_back(grad_normed, unit_one, scale_one, gain_attn)
    grad_tokens = (grad_residual + grad_from_attn).astype(jnp.bfloat16)
    shares = (
        lax.psum_scatter(
            grad_query_w.astype(jnp.bfloat16), "fsdp", scatter_dimension=0, tiled=True
        ).astype(jnp.float32),
        lax.psum_scatter(
            grad_key_w.astype(jnp.bfloat16), "fsdp", scatter_dimension=0, tiled=True
        ).astype(jnp.float32),
        lax.psum_scatter(
            grad_value_w.astype(jnp.bfloat16), "fsdp", scatter_dimension=0, tiled=True
        ).astype(jnp.float32),
        lax.psum_scatter(
            grad_output_w.astype(jnp.bfloat16), "fsdp", scatter_dimension=0, tiled=True
        ).astype(jnp.float32),
        lax.psum_scatter(
            grad_router_w.astype(jnp.bfloat16), "fsdp", scatter_dimension=0, tiled=True
        ).astype(jnp.float32),
        lax.psum_scatter(
            grad_gain_attn.astype(jnp.bfloat16), "fsdp", scatter_dimension=0, tiled=True
        ).astype(jnp.float32),
        lax.psum_scatter(
            grad_gain_ffn.astype(jnp.bfloat16), "fsdp", scatter_dimension=0, tiled=True
        ).astype(jnp.float32),
        lax.psum_scatter(
            grad_rel.astype(jnp.bfloat16), "fsdp", scatter_dimension=0, tiled=True
        ).astype(jnp.float32),
    )
    summed = lax.psum(
        (shares[0], shares[1], shares[2], shares[3], shares[4], shares[5], shares[6], shares[7]),
        "dp",
    )
    return (
        layer_out,
        grad_tokens,
        summed[0],
        summed[1],
        summed[2],
        summed[3],
        summed[4],
        summed[5],
        summed[6],
        summed[7],
        grad_first,
        grad_second,
    )


def solution(mesh):
    placed = (
        P(("fsdp", "dp"), None),
        P(("fsdp", "dp"), None),
        P(("fsdp", "dp"), None),
        P(("fsdp", "dp"), None),
        P(),
        P("fsdp", None),
        P("fsdp", None),
        P("fsdp", None),
        P("fsdp", None),
        P("fsdp", None),
        P("fsdp"),
        P("fsdp"),
        P("fsdp", None),
        P("dp", None, "fsdp"),
        P("dp", "fsdp", None),
    )
    return jax.shard_map(
        local,
        mesh=mesh,
        in_specs=placed,
        out_specs=(
            P(("fsdp", "dp"), None),
            P(("fsdp", "dp"), None),
            P("fsdp", None),
            P("fsdp", None),
            P("fsdp", None),
            P("fsdp", None),
            P("fsdp", None),
            P("fsdp"),
            P("fsdp"),
            P("fsdp", None),
            P("dp", None, "fsdp"),
            P("dp", "fsdp", None),
        ),
        check_vma=False,
    )
```

profile of v0, /device:TPU:0, one launch (start us, length us, event | category | flops | bytes accessed | tf_op | source)
XLA Modules:
  0.0 698.3 jit_solution(5562469548196357077)
XLA Ops:
  13.8 8.3 %all-reduce.11 = (bf16[768]{0:T(1024)(128)(2,1)S(1)}, bf16[768]{0:T(1024)(128)(2,1)S(1)}) all-reduce(bf16[768]{0:T(1024)(128)(2,1)S(1)} %dynamic-update-slice, bf16[768]{0:T(1024)(128)(2,1)S(1)} %dynamic-update-slice.1), channel_id=1, replica_groups=mesh['fsdp'=4,'dp'=8] {'fsdp'}, use_global_device_ids=true, to_apply=%add.4 | all-reduce | flops 1536 | bytes 6144
  27.9 11.9 %tile.4 = f32[12,512,1024]{2,1,0:T(8,128)} broadcast(f32[12,1024]{1,0:T(8,128)S(1)} %maximum_bitcast_fusion), dimensions={0,2} | broadcast | bytes 25214976 | tf_op jit(solution)/shard_map/jvp()/tile | solution.py:41
  39.8 10.9 %pad.22 = f32[16,512,1024]{2,1,0:T(8,128)S(1)} pad(f32[12,512,1024]{2,1,0:T(8,128)} %tile.4, f32[]{:T(128)} %constant.9.clone.1), padding=0_4x0_0x0_0 | pad | bytes 58720260
  50.8 39.7 %copy.80 = f32[2,8,512,1024]{3,1,2,0:T(8,128)} copy(f32[2,8,512,1024]{3,2,1,0:T(8,128)S(1)} %bitcast.102) | data formatting | bytes 67108864
  90.5 23.1 %slice.20 = f32[12,523776]{1,0:T(8,128)} slice(f32[12,524288]{1,0:T(8,128)} %bitcast.104), slice={[0:12], [0:523776]} | slice | bytes 50282496 | tf_op jit(solution)/shard_map/jvp()/slice | solution.py:41
  113.5 51.1 %reshape.198 = f32[12,512,1023]{2,1,0:T(8,128)} reshape(f32[12,523776]{1,0:T(8,128)} %slice.20) | data formatting | bytes 50282496 | tf_op jit(solution)/shard_map/jvp()/reshape | solution.py:42
  164.6 10.7 %slice.21 = f32[12,512,512]{2,1,0:T(8,128)} slice(f32[12,512,1023]{2,1,0:T(8,128)} %reshape.198), slice={[0:12], [0:512], [0:512]} | slice | bytes 25165824 | tf_op jit(solution)/shard_map/jvp()/slice | solution.py:42
  175.3 12.6 %copy.78 = f32[12,512,512]{1,2,0:T(8,128)} copy(f32[12,512,512]{2,1,0:T(8,128)} %slice.21) | data formatting | bytes 25165824
  197.4 6.1 fusion.97
  214.9 6.3 all-to-all-start
  221.2 5.2 all-gather
  229.2 29.4 %all-to-all-done = bf16[8,128,768]{2,1,0:T(8,128)(2,1)} async-done(((bf16[8,128,768]{2,1,0:T(8,128)(2,1)}), bf16[8,128,768]{2,1,0:T(8,128)(2,1)}, u32[]{:S(2)}, u32[]{:S(2)}) %all-to-all-start) | async-done | bytes 1572896 | tf_op jit(solution)/shard_map/all_to_all | solution.py:146
  263.0 10.1 %fusion.14 = f32[1024,3072]{1,0:T(8,128)} fusion(bf16[1024,768]{1,0:T(8,128)(2,1)} %bitcast.12, bf16[1,768,3072]{2,1,0:T(8,128)(2,1)} %all-gather.16.cloned.1.call-done), kind=kOutput, calls=%fused_computation.26 | convolution fusion | flops 4831838208 | bytes 18874368 | tf_op jit(solution)/shard_map/dot_general | solution.py:155
  273.1 12.5 %fusion.33 = bf16[1024,768]{1,0:T(8,128)(2,1)} fusion(bf16[1,3072,768]{2,1,0:T(8,128)(2,1)} %all-gather.18.cloned.1.call-done, f32[1024,3072]{1,0:T(8,128)} %fusion.14), kind=kOutput, calls=%fused_computation.48 | convolution fusion | flops 4860936192 | bytes 18874368 | tf_op jit(solution)/shard_map/dot_general | solution.py:157
  285.6 14.0 %all-to-all-done.2 = bf16[8,128,768]{2,1,0:T(8,128)(2,1)} async-done(((bf16[8,128,768]{2,1,0:T(8,128)(2,1)}), bf16[8,128,768]{2,1,0:T(8,128)(2,1)}, u32[]{:S(2)}, u32[]{:S(2)}) %all-to-all-start.2) | async-done | bytes 1572896 | tf_op jit(solution)/shard_map/all_to_all | solution.py:171
  304.3 15.4 %fusion.6 = bf16[1024,3072]{1,0:T(8,128)(2,1)S(1)} fusion(f32[1024,3072]{1,0:T(8,128)} %fusion.14, bf16[1024,768]{1,0:T(8,128)(2,1)} %bitcast.18, bf16[1,3072,768]{2,1,0:T(8,128)(2,1)} %all-gather.18.cloned.1.call-done), kind=kOutput, calls=%fused_computation.10 | convolution fusion | flops 4894752768 | bytes 25165824 | tf_op jit(solution)/shard_map/dot_general | solution.py:174
  322.3 8.5 %fusion.30 = bf16[1024,768]{1,0:T(8,128)(2,1)} fusion(bf16[1024,3072]{1,0:T(8,128)(2,1)S(1)} %fusion.6, bf16[1,768,3072]{2,1,0:T(8,128)(2,1)} %all-gather.16.cloned.1.call-done), kind=kOutput, calls=%fused_computation.47 | convolution fusion | flops 4832624640 | bytes 12582912 | tf_op jit(solution)/shard_map/dot_general | solution.py:176
  330.9 10.0 %all-to-all-done.1 = bf16[8,128,768]{2,1,0:T(8,128)(2,1)} async-done(((bf16[8,128,768]{2,1,0:T(8,128)(2,1)}), bf16[8,128,768]{2,1,0:T(8,128)(2,1)}, u32[]{:S(2)}, u32[]{:S(2)}) %all-to-all-start.1) | async-done | bytes 1572896 | tf_op jit(solution)/shard_map/all_to_all | solution.py:160
  351.3 30.5 %all-to-all-done.3 = bf16[8,128,768]{2,1,0:T(8,128)(2,1)} async-done(((bf16[8,128,768]{2,1,0:T(8,128)(2,1)}), bf16[8,128,768]{2,1,0:T(8,128)(2,1)}, u32[]{:S(2)}, u32[]{:S(2)}) %all-to-all-start.3) | async-done | bytes 1572896 | tf_op jit(solution)/shard_map/all_to_all | solution.py:189
  394.1 7.2 %fusion.54 = bf16[12,64,512]{2,1,0:T(8,128)(2,1)S(1)} fusion(bf16[512,12,64]{0,2,1:T(8,128)(2,1)} %bitcast.110, f32[12,512,512]{1,2,0:T(8,128)} %copy-done, f32[12,512]{1,0:T(8,128)S(1)} %log_add_fusion), kind=kOutput, calls=%fused_computation.77 | convolution fusion | flops 409337856 | bytes 14180352 | tf_op jit(solution)/shard_map/hqk,qhd->khd/dot_general | solution.py:220
  404.2 6.4 multiply_reduce_fusion
  410.6 6.9 multiply_convert_fusion
  431.1 12.2 %fusion.17 = bf16[1,3072,768]{2,1,0:T(8,128)(2,1)} fusion(bf16[1024,768]{1,0:T(8,128)(2,1)} %bitcast.18, f32[1024,3072]{1,0:T(8,128)} %fusion.14), kind=kOutput, calls=%fused_computation.29 | convolution fusion | flops 4862509056 | bytes 18874368 | tf_op jit(solution)/shard_map/dot_general | solution.py:180
  444.7 9.2 %fusion.16 = bf16[1,768,3072]{2,1,0:T(8,128)(2,1)} fusion(bf16[1024,768]{1,0:T(8,128)(2,1)} %bitcast.12, bf16[1024,3072]{1,0:T(8,128)(2,1)} %copy-done.32), kind=kOutput, calls=%fused_computation.28 | convolution fusion | flops 4834197504 | bytes 12582912 | tf_op jit(solution)/shard_map/dot_general | solution.py:179
  453.9 8.7 %copy.79 = bf16[12,512,512]{2,1,0:T(8,128)(2,1)} copy(bf16[12,512,512]{1,2,0:T(8,128)(2,1)} %copy-done.1) | data formatting | bytes 12582912
  462.6 9.0 %pad.16.clone = bf16[12,512,1023]{2,1,0:T(8,128)(2,1)} pad(bf16[12,512,512]{2,1,0:T(8,128)(2,1)} %copy.79, bf16[]{:T(256)} %constant.37.clone.1), padding=0_0x0_0x0_511 | pad | bytes 18862082 | tf_op jit(solution)/shard_map/transpose(jvp())/pad | solution.py:42
  471.6 35.2 %reshape.212 = bf16[12,523776]{1,0:T(8,128)(2,1)} reshape(bf16[12,512,1023]{2,1,0:T(8,128)(2,1)} %pad.16.clone) | data formatting | bytes 25141248 | tf_op jit(solution)/shard_map/transpose(jvp())/reshape | solution.py:42
  506.8 9.5 %pad_convert_fusion = f32[12,524288]{1,0:T(8,128)S(1)} fusion(bf16[12,523776]{1,0:T(8,128)(2,1)} %reshape.212), kind=kLoop, calls=%fused_computation.3 | loop fusion | flops 6291456 | bytes 37736448 | tf_op jit(solution)/shard_map/transpose(jvp())/reshape | solution.py:41
  516.3 35.8 %copy.81 = f32[2,8,512,1024]{3,2,1,0:T(8,128)} copy(f32[2,8,512,1024]{3,1,2,0:T(8,128)S(1)} %bitcast.103) | data formatting | bytes 67108864
  552.1 11.2 %slice_reduce_fusion = f32[12,1024]{1,0:T(8,128)S(1)} fusion(f32[16,512,1024]{2,1,0:T(8,128)} %bitcast.105), kind=kLoop, calls=%fused_computation | loop fusion | flops 6279168 | bytes 25214976 | tf_op jit(solution)/shard_map/transpose(jvp())/reduce_sum | solution.py:41
  569.4 11.1 %all-reduce.10 = (bf16[768]{0:T(1024)(128)(2,1)S(1)}, bf16[768]{0:T(1024)(128)(2,1)S(1)}, bf16[32,12]{1,0:T(8,128)(2,1)S(1)}) all-reduce(bf16[768]{0:T(1024)(128)(2,1)S(1)} %get-tuple-element.14, bf16[768]{0:T(1024)(128)(2,1)S(1)} %get-tuple-element.12, ...), channel_id=7, replica_groups=mesh['fsdp'=4,'dp'=8] {'fsdp'}, use_global_device_ids=true, to_apply=%region_25.26.clone | all-reduce | flops 1920 | bytes 7680
  584.2 101.7 %all-reduce.13 = (f32[192,768]{1,0:T(8,128)}, f32[192,768]{1,0:T(8,128)}, f32[192,768]{1,0:T(8,128)}, f32[192,768]{1,0:T(8,128)}, f32[192,8]{0,1:T(8,128)}, /*in...) all-reduce(bf16[192,768]{1,0:T(8,128)(2,1)} %reduce-scatter.10.cloned.1., ...), channel_id=1, replica_groups=mesh['fsdp'=4,'dp'=8] {'dp'}, use_global_device_ids=true, to_apply=%region_15.16 | all-reduce | flops 591840 | bytes 3552000 | tf_op jit(solution)/shard_map/psum | solution.py:274
  (172 shorter events, 101.3 us)
Async XLA Ops:
  7.2 180.7 %all-gather.10.cloned.1.call-start = ((), (), s32[]{:S(2)}) async-start(), calls=%async_computation.12 | async-start | bytes 1474560 | tf_op jit(solution)/shard_map/all_gather | solution.py:81
  7.9 3.6 copy-start.21
  7.9 182.4 %all-gather.12.cloned.1.call-start = ((), (), s32[]{:S(2)}) async-start(), calls=%async_computation.13 | async-start | bytes 1474560 | tf_op jit(solution)/shard_map/all_gather | solution.py:82
  8.7 184.3 %all-gather.8.cloned.1.call-start = ((), (), s32[]{:S(2)}) async-start(), calls=%async_computation.11 | async-start | bytes 1474560 | tf_op jit(solution)/shard_map/all_gather | solution.py:83
  9.4 200.6 %all-gather.14.cloned.1.call-start = ((), (), s32[]{:S(2)}) async-start(), calls=%async_computation.14 | async-start | bytes 1474560 | tf_op jit(solution)/shard_map/all_gather | solution.py:84
  10.0 3.5 copy-start.31
  10.0 12.1 %copy-start.23 = (bf16[8,12]{1,0:T(8,128)(2,1)S(1)}, bf16[8,12]{1,0:T(8,128)(2,1)}, u32[]{:S(2)}) copy-start(bf16[8,12]{1,0:T(8,128)(2,1)} %param.27) | copy-start | bytes 580
  10.0 17.3 %copy-start.27 = (s32[1024]{0:T(1024)S(1)}, s32[1024]{0:T(1024)}, u32[]{:S(2)}) copy-start(s32[1024]{0:T(1024)} %param.19) | copy-start | bytes 12292
  10.1 252.9 %all-gather.16.cloned.1.call-start = ((), (), s32[]{:S(2)}) async-start(), calls=%async_computation.15 | async-start | bytes 5898240 | tf_op jit(solution)/shard_map/all_gather | solution.py:150
  10.6 262.4 %all-gather.18.cloned.1.call-start = ((), (), s32[]{:S(2)}) async-start(), calls=%async_computation.16 | async-start | bytes 5898240 | tf_op jit(solution)/shard_map/all_gather | solution.py:151
  190.3 7.1 %copy-start.5 = (bf16[512,768]{0,1:T(8,128)(2,1)}, bf16[512,768]{0,1:T(8,128)(2,1)S(1)}, u32[]{:S(2)}) copy-start(bf16[512,768]{0,1:T(8,128)(2,1)S(1)} %copy.62) | copy-start | bytes 2359300
  203.5 4.5 copy-start
  214.9 6.3 copy-start.22
  214.9 12.0 %copy-start.17 = (bf16[512,768]{1,0:T(8,128)(2,1)S(1)}, bf16[512,768]{1,0:T(8,128)(2,1)}, u32[]{:S(2)}) copy-start(bf16[512,768]{1,0:T(8,128)(2,1)} %param.16) | copy-start | bytes 2359300
  214.9 43.7 %all-to-all-start = ((bf16[8,128,768]{2,1,0:T(8,128)(2,1)}), bf16[8,128,768]{2,1,0:T(8,128)(2,1)}, u32[]{:S(2)}, u32[]{:S(2)}) async-start(bf16[8,128,768]{2,1,0:T(8,128)(2,1)} %bitcast.122), calls=%async_computation | async-start | bytes 3145728 | tf_op jit(solution)/shard_map/all_to_all | solution.py:146
  258.6 40.9 %all-to-all-start.2 = ((bf16[8,128,768]{2,1,0:T(8,128)(2,1)}), bf16[8,128,768]{2,1,0:T(8,128)(2,1)}, u32[]{:S(2)}, u32[]{:S(2)}) async-start(bf16[8,128,768]{2,1,0:T(8,128)(2,1)} %bitcast.121), calls=%async_computation.2 | async-start | bytes 3145728 | tf_op jit(solution)/shard_map/all_to_all | solution.py:171
  299.6 41.3 %all-to-all-start.1 = ((bf16[8,128,768]{2,1,0:T(8,128)(2,1)}), bf16[8,128,768]{2,1,0:T(8,128)(2,1)}, u32[]{:S(2)}, u32[]{:S(2)}) async-start(bf16[8,128,768]{2,1,0:T(8,128)(2,1)} %bitcast.123), calls=%async_computation.1 | async-start | bytes 3145728 | tf_op jit(solution)/shard_map/all_to_all | solution.py:160
  340.9 40.9 %all-to-all-start.3 = ((bf16[8,128,768]{2,1,0:T(8,128)(2,1)}), bf16[8,128,768]{2,1,0:T(8,128)(2,1)}, u32[]{:S(2)}, u32[]{:S(2)}) async-start(bf16[8,128,768]{2,1,0:T(8,128)(2,1)} %bitcast.120), calls=%async_computation.3 | async-start | bytes 3145728 | tf_op jit(solution)/shard_map/all_to_all | solution.py:189
  345.2 238.1 %reduce-scatter.22.cloned.1.call-start = ((), (), s32[]{:S(2)}) async-start(), calls=%async_computation.23 | async-start | bytes 245760
  350.2 234.0 %reduce-scatter.16.cloned.1.call-start = ((), (), s32[]{:S(2)}) async-start(), calls=%async_computation.20 | async-start | bytes 1474560 | tf_op jit(solution)/shard_map/reduce_scatter | solution.py:258
  381.8 3.5 copy-start.15
  381.8 3.5 copy-start.18
  388.6 195.5 %reduce-scatter.14.cloned.1.call-start = ((), (), s32[]{:S(2)}) async-start(), calls=%async_computation.19 | async-start | bytes 1474560 | tf_op jit(solution)/shard_map/reduce_scatter | solution.py:255
  394.1 8.0 %copy-start.3 = (bf16[512,768]{1,0:T(8,128)(2,1)S(1)}, bf16[512,768]{1,0:T(8,128)(2,1)}, u32[]{:S(2)}) copy-start(bf16[512,768]{1,0:T(8,128)(2,1)} %param.15) | copy-start | bytes 2359300
  404.1 180.1 %reduce-scatter.10.cloned.1.call-start = ((), (), s32[]{:S(2)}) async-start(), calls=%async_computation.17 | async-start | bytes 1474560 | tf_op jit(solution)/shard_map/reduce_scatter | solution.py:249
  417.5 3.5 copy-start.4
  423.0 161.3 %reduce-scatter.12.cloned.1.call-start = ((), (), s32[]{:S(2)}) async-start(), calls=%async_computation.18 | async-start | bytes 1474560 | tf_op jit(solution)/shard_map/reduce_scatter | solution.py:252
  431.1 254.8 %reduce-scatter.20.cloned.1.call-start = ((), (), s32[]{:S(2)}) async-start(), calls=%async_computation.22 | async-start | bytes 5898240 | tf_op jit(solution)/shard_map/reduce_scatter | solution.py:185
  443.4 245.4 %reduce-scatter.18.cloned.1.call-start = ((), (), s32[]{:S(2)}) async-start(), calls=%async_computation.21 | async-start | bytes 5898240 | tf_op jit(solution)/shard_map/reduce_scatter | solution.py:182
  552.1 11.3 %copy-start.28 = (s32[1024]{0:T(1024)S(1)}, s32[1024]{0:T(1024)}, u32[]{:S(2)}) copy-start(s32[1024]{0:T(1024)} %param.19) | copy-start | bytes 12292
  552.1 11.9 %copy-start.14 = (bf16[12,64,512]{2,1,0:T(8,128)(2,1)S(1)}, bf16[12,64,512]{2,1,0:T(8,128)(2,1)}, u32[]{:S(2)}) copy-start(bf16[12,64,512]{2,1,0:T(8,128)(2,1)} %copy-done.13) | copy-start | bytes 2359300
  552.1 11.9 %copy-start.25 = (bf16[768,768]{1,0:T(8,128)(2,1)S(1)}, bf16[768,768]{1,0:T(8,128)(2,1)}, u32[]{:S(2)}) copy-start(bf16[768,768]{1,0:T(8,128)(2,1)} %all-gather.10.cloned.1.call-done) | copy-start | bytes 3538948
  (18 other events, 37.1 us)
Sparse Core Ops, SparseCore 0:
  9.6 20.2 all-gather.9
  31.4 17.4 all-gather.11
  50.5 17.4 all-gather.7
  69.4 17.4 all-gather.13
  88.3 37.4 all-gather.15
  127.2 37.4 all-gather.17
  350.3 20.3 reduce-scatter.21
  388.8 24.0 reduce-scatter.15
  415.6 25.7 reduce-scatter.13
  444.4 25.6 reduce-scatter.9
  472.8 25.7 reduce-scatter.11
  501.0 47.8 reduce-scatter.19
  551.5 48.1 reduce-scatter.17
where the time goes:
time: 708 us; the launch traced here: 698 us
  local copies, waits for them, and re-layouts  267 us (38%)
  matrix products  135 us (19%)
  blocking collectives  131 us (19%)
  waiting for transfers between devices  87.8 us (12%)
  other arithmetic  40.5 us (6%)
  starting transfers between devices  20.5 us (3%)
  between operations  16.7 us (2%)
    unnamed x79, local copies, waits for them, and re-layouts  121 us
    psum x1, blocking collectives, local(): lax.psum((shares[0], shares[1], shares[2], shares[3], shares[4], shares[5...  102 us
    reshape x2, local copies, waits for them, and re-layouts, relative_bias(): return flat.reshape(heads_n, tok_rows, span)[:, :, :tok_rows]  86.3 us
    all_to_all x1, waiting for transfers between devices, local(): lax.all_to_all(grad_expert_rows.reshape(experts, capacity, D), 'dp', spli...  30.5 us
    all_to_all x1, waiting for transfers between devices, local(): lax.all_to_all(send_rows.reshape(experts, capacity, D), 'dp', split_axis=...  29.4 us
    slice x1, local copies, waits for them, and re-layouts, relative_bias(): flat = jnp.tile(per_head, (1, tok_rows))[:, :tok_rows * span]  23.1 us
    unnamed x2, blocking collectives  19.4 us
    dot_general x1, matrix products, local(): jnp.dot(grad_arrived, second_w.T, preferred_element_type=jnp.float32)  15.4 us
  transfers between devices with their start and end apart: 17, of which 4 were waited for; matrix products, arithmetic and copies ran while one was open for 61% of the time, Pallas kernels for 0%

commit v1 on v0

v1 whole, which is shorter than its diff:
```python
import jax
import jax.numpy as jnp
from jax import lax
from jax.experimental import pallas as pl
from jax.experimental.pallas import tpu as pltpu
from jax.sharding import PartitionSpec as P

D = 768
HEADS = 12
HEAD_DIM = 64
PAIR = 2 * HEAD_DIM
BAND = 128

EPSILON = 1e-06
PRECISE = lax.Precision.HIGHEST
MASKED = -1e30
F32 = jnp.float32
LOW = jnp.bfloat16


def norm_parts(values, gain_vec):
    scale_row = lax.rsqrt(jnp.mean(values * values, axis=-1, keepdims=True) + EPSILON)
    unit_rows = values * scale_row
    return (unit_rows * gain_vec, unit_rows, scale_row)


def norm_back(grad_rows, unit_rows, scale_row, gain_vec):
    gain_grad = jnp.sum(grad_rows * unit_rows, axis=0)
    scaled = grad_rows * gain_vec
    return (
        scale_row * (scaled - unit_rows * jnp.mean(scaled * unit_rows, axis=-1, keepdims=True)),
        gain_grad,
    )


def dot_nt(a, b):
    return lax.dot_general(a, b, (((1,), (1,)), ((), ())), preferred_element_type=F32)


def dot_tn(a, b):
    return lax.dot_general(a, b, (((0,), (0,)), ((), ())), preferred_element_type=F32)


def dot_nn(a, b):
    return jnp.dot(a, b, preferred_element_type=F32)


def attend_kernel(q_ref, k_ref, v_ref, offs_ref, seg_col_ref, seg_row_ref, out_ref, attn_ref):
    rows = q_ref.shape[0]
    span = 2 * rows
    same_seq = seg_col_ref[...] == seg_row_ref[...]
    for h in range(2):
        cols = slice(h * HEAD_DIM, (h + 1) * HEAD_DIM)
        wide = jnp.broadcast_to(offs_ref[h], (BAND, span))
        wide = pltpu.roll(wide, 0, 1, stride=1, stride_axis=0)
        for b in range(rows // BAND):
            part = slice(b * BAND, (b + 1) * BAND)
            start = (span - b * BAND) % span
            if start + rows <= span:
                bias = wide[:, start : start + rows]
            else:
                bias = jnp.concatenate(
                    [wide[:, start:], wide[:, : start + rows - span]], axis=1
                )
            scores = dot_nt(q_ref[part, cols], k_ref[:, cols]) + bias
            scores = jnp.where(same_seq[part], scores, MASKED)
            top = jnp.max(scores, axis=-1, keepdims=True)
            raised = jnp.exp(scores - top)
            total = jnp.sum(raised, axis=-1, keepdims=True)
            attn = (raised * (1.0 / total)).astype(LOW)
            attn_ref[h, part, :] = attn
            out_ref[part, cols] = dot_nn(attn, v_ref[:, cols]).astype(LOW)


def attend(qkv, offs, segment):
    rows = qkv.shape[0]
    pairs = HEADS // 2
    block = (rows, PAIR)
    return pl.pallas_call(
        attend_kernel,
        grid=(pairs,),
        in_specs=[
            pl.BlockSpec(block, lambda p: (0, p)),
            pl.BlockSpec(block, lambda p: (0, pairs + p)),
            pl.BlockSpec(block, lambda p: (0, 2 * pairs + p)),
            pl.BlockSpec((2, 1, 2 * rows), lambda p: (p, 0, 0)),
            pl.BlockSpec((rows, 1), lambda p: (0, 0)),
            pl.BlockSpec((1, rows), lambda p: (0, 0)),
        ],
        out_specs=[
            pl.BlockSpec(block, lambda p: (0, p)),
            pl.BlockSpec((2, rows, rows), lambda p: (p, 0, 0)),
        ],
        out_shape=[
            jax.ShapeDtypeStruct((rows, HEADS * HEAD_DIM), LOW),
            jax.ShapeDtypeStruct((HEADS, rows, rows), LOW),
        ],
        compiler_params=pltpu.CompilerParams(vmem_limit_bytes=40 * 1024 * 1024),
        cost_estimate=pl.CostEstimate(
            flops=4 * HEADS * rows * rows * HEAD_DIM,
            bytes_accessed=4 * rows * HEADS * HEAD_DIM * 2 + HEADS * rows * rows * 2,
            transcendentals=HEADS * rows * rows,
        ),
    )(qkv, qkv, qkv, offs, segment[:, None], segment[None, :])


def attend_back_kernel(q_ref, k_ref, v_ref, go_ref, attn_ref, gq_ref, gk_ref, gv_ref, diag_ref):
    rows = q_ref.shape[0]
    span = 2 * rows
    bands = rows // BAND
    down = lax.broadcasted_iota(jnp.int32, (BAND, BAND), 0)
    upside = (down + lax.broadcasted_iota(jnp.int32, (BAND, BAND), 1) == BAND - 1).astype(F32)
    for h in range(2):
        cols = slice(h * HEAD_DIM, (h + 1) * HEAD_DIM)
        pieces = [None] * (span // BAND)
        grad_parts = []
        for b in range(bands):
            part = slice(b * BAND, (b + 1) * BAND)
            attn = attn_ref[h, part, :].astype(F32)
            grad_attn = dot_nt(go_ref[part, cols], v_ref[:, cols])
            mean = jnp.sum(attn * grad_attn, axis=-1, keepdims=True)
            grad = (attn * (grad_attn - mean)).astype(LOW)
            grad_parts.append(grad)
            gq_ref[part, cols] = dot_nn(grad, k_ref[:, cols]).astype(LOW)
            grad_f = grad.astype(F32)
            for c in range(bands):
                at = (c - b) % (span // BAND)
                piece = grad_f[:, c * BAND : (c + 1) * BAND]
                pieces[at] = piece if pieces[at] is None else pieces[at] + piece
        grads = jnp.concatenate(grad_parts, axis=0)
        gk_ref[:, cols] = dot_tn(grads, q_ref[:, cols]).astype(LOW)
        gv_ref[:, cols] = dot_tn(attn_ref[h], go_ref[:, cols]).astype(LOW)
        pieces = [jnp.zeros((BAND, BAND), F32) if x is None else x for x in pieces]
        wide = jnp.concatenate(pieces, axis=1)
        wide = jnp.dot(upside, wide, precision=PRECISE, preferred_element_type=F32)
        wide = pltpu.roll(wide, span - BAND + 1, 1, stride=1, stride_axis=0)
        diag_ref[h] = jnp.sum(wide, axis=0, keepdims=True)


def attend_back(qkv, grad_attended, attn_low):
    rows = qkv.shape[0]
    pairs = HEADS // 2
    block = (rows, PAIR)
    flat = jax.ShapeDtypeStruct((rows, HEADS * HEAD_DIM), LOW)
    return pl.pallas_call(
        attend_back_kernel,
        grid=(pairs,),
        in_specs=[
            pl.BlockSpec(block, lambda p: (0, p)),
            pl.BlockSpec(block, lambda p: (0, pairs + p)),
            pl.BlockSpec(block, lambda p: (0, 2 * pairs + p)),
            pl.BlockSpec(block, lambda p: (0, p)),
            pl.BlockSpec((2, rows, rows), lambda p: (p, 0, 0)),
        ],
        out_specs=[
            pl.BlockSpec(block, lambda p: (0, p)),
            pl.BlockSpec(block, lambda p: (0, p)),
            pl.BlockSpec(block, lambda p: (0, p)),
            pl.BlockSpec((2, 1, 2 * rows), lambda p: (p, 0, 0)),
        ],
        out_shape=[flat, flat, flat, jax.ShapeDtypeStruct((HEADS, 1, 2 * rows), F32)],
        compiler_params=pltpu.CompilerParams(vmem_limit_bytes=40 * 1024 * 1024),
        cost_estimate=pl.CostEstimate(
            flops=8 * HEADS * rows * rows * HEAD_DIM,
            bytes_accessed=7 * rows * HEADS * HEAD_DIM * 2 + HEADS * rows * rows * 2,
            transcendentals=0,
        ),
    )(qkv, qkv, qkv, grad_attended, attn_low)


def swap(rows, experts):
    return lax.all_to_all(
        rows.reshape(experts, -1, rows.shape[-1]), "dp", split_axis=0, concat_axis=0, tiled=True
    ).reshape(rows.shape)


def group_sum(grads):
    share = lax.psum_scatter(grads, "fsdp", scatter_dimension=0, tiled=True)
    return lax.psum(share, "dp").astype(F32)


def in_column(values, rows):
    flat = values.reshape(-1, 1)
    return jnp.pad(flat, ((0, rows - flat.shape[0]), (0, 0)))


def local(
    tokens,
    cotangent,
    seq_lengths,
    routes,
    bucket_table,
    w_query,
    w_key,
    w_value,
    w_output,
    w_router,
    norm_attn,
    norm_ffn,
    rel_bias,
    expert_in,
    expert_out,
):
    tok_rows = tokens.shape[0]
    experts = lax.axis_size("dp")
    groups = lax.axis_size("fsdp")
    capacity = 2 * tok_rows // experts
    slots = experts * capacity
    share = w_query.shape[0]
    buckets_own = rel_bias.shape[0]
    buckets = buckets_own * groups
    wide = HEADS * HEAD_DIM
    small = -(-(experts + 3) // 128) * 128
    pack = jnp.concatenate(
        [
            w_query,
            w_key,
            w_value,
            w_output,
            w_router,
            norm_attn[:, None],
            norm_ffn[:, None],
            in_column(rel_bias, share),
            jnp.zeros((share, small - experts - 3), LOW),
        ],
        axis=1,
    )
    packed = lax.all_gather(pack, "fsdp", axis=0, tiled=True)
    qkv_w = packed[:, : 3 * wide]
    output_w = packed[:, 3 * wide : 3 * wide + D]
    rest = packed[:, 3 * wide + D :]
    router_w = rest[:, :experts]
    gain_attn = rest[:, experts].astype(F32)
    gain_ffn = rest[:, experts + 1].astype(F32)
    rel_table = (
        rest[:, experts + 2]
        .reshape(groups, share)[:, : buckets_own * HEADS]
        .reshape(buckets, HEADS)
    )
    first_w = lax.all_gather(expert_in[0], "fsdp", axis=1, tiled=True)
    second_w = lax.all_gather(expert_out[0], "fsdp", axis=0, tiled=True)

    route_ids = routes[:, 0]
    position = jnp.arange(tok_rows, dtype=jnp.int32)
    chosen = (route_ids[:, None] == jnp.arange(experts, dtype=jnp.int32)[None, :]).astype(F32)
    lower_tri = (position[:, None] > position[None, :]).astype(LOW)
    earlier = dot_nn(lower_tri, chosen.astype(LOW))
    slot_rank = jnp.sum(earlier * chosen, axis=1).astype(jnp.int32)
    slot_index = route_ids * capacity + slot_rank
    slot_ids = jnp.arange(slots, dtype=jnp.int32)
    slot_hot = (slot_ids[:, None] == slot_index[None, :]).astype(LOW)
    cot_arrived = swap(dot_nn(slot_hot, cotangent).astype(LOW), experts)

    ends_at = jnp.cumsum(seq_lengths[0])
    segment = jnp.sum((position[:, None] >= ends_at[None, :]).astype(jnp.int32), axis=1)
    inputs_f = tokens.astype(F32)
    normed_f, unit_one, scale_one = norm_parts(inputs_f, gain_attn)
    normed = normed_f.astype(LOW)
    qkv = dot_nn(normed, qkv_w).astype(LOW)
    rolled = jnp.roll(bucket_table, -tok_rows)
    bucket_hot = rolled[None, :] == jnp.arange(buckets, dtype=jnp.int32)[:, None]
    offs = dot_tn(rel_table, bucket_hot.astype(LOW))[:, None, :]
    attended, attn_low = attend(qkv, offs, segment)
    residual = inputs_f + dot_nn(attended, output_w)
    ffn_f, unit_two, scale_two = norm_parts(residual, gain_ffn)
    ffn_in = ffn_f.astype(LOW)
    router_p = jax.nn.softmax(dot_nn(ffn_in, router_w), axis=-1)
    gate_value = jnp.sum(router_p * chosen, axis=-1, keepdims=True)
    arrived = swap(dot_nn(slot_hot, ffn_in).astype(LOW), experts)

    own = (jnp.arange(experts, dtype=jnp.int32) == lax.axis_index("dp")).astype(F32)[None, :]
    router_there = jax.nn.softmax(dot_nn(arrived, router_w), axis=-1)
    gate_there = jnp.sum(router_there * own, axis=-1, keepdims=True)
    cot_f = cot_arrived.astype(F32)
    grad_arrived = (gate_there * cot_f).astype(LOW)
    hidden_pre = dot_nn(arrived, first_w)
    hidden_f, pull_back = jax.vjp(jax.nn.gelu, hidden_pre)
    hidden_act = hidden_f.astype(LOW)
    expert_result = dot_nn(hidden_act, second_w).astype(LOW)
    grad_gate = jnp.sum(cot_f * expert_result.astype(F32), axis=-1, keepdims=True)
    grad_logits = router_there * (own - gate_there) * grad_gate
    grad_pre = pull_back(dot_nt(grad_arrived, second_w))[0].astype(LOW)
    grad_rows = dot_nt(grad_pre, first_w) + jnp.dot(
        grad_logits, router_w.astype(F32).T, precision=PRECISE
    )
    grad_back = swap(grad_rows.astype(LOW), experts)
    first_term = dot_tn(arrived, grad_pre).astype(LOW)
    second_term = dot_tn(hidden_act, grad_arrived).astype(LOW)
    grad_first = lax.psum_scatter(first_term, "fsdp", scatter_dimension=1, tiled=True)
    grad_second = lax.psum_scatter(second_term, "fsdp", scatter_dimension=0, tiled=True)
    grad_router_w = jnp.dot(arrived.astype(F32).T, grad_logits, precision=PRECISE)
    expert_result, grad_back = lax.optimization_barrier((expert_result, grad_back))
    returned = swap(expert_result, experts)

    grad_out = cotangent.astype(F32)
    grad_ffn_in = dot_tn(slot_hot, grad_back)
    grad_from_ffn, grad_gain_ffn = norm_back(grad_ffn_in, unit_two, scale_two, gain_ffn)
    grad_residual = grad_out + grad_from_ffn
    grad_att = grad_residual.astype(LOW)
    grad_attended = dot_nt(grad_att, output_w).astype(LOW)
    grad_q, grad_k, grad_v, diag = attend_back(qkv, grad_attended, attn_low)
    grad_output_w = dot_tn(attended, grad_att)
    grad_rel = dot_general_buckets(bucket_hot, diag[:, 0, :])
    grad_qkv = jnp.concatenate([grad_q, grad_k, grad_v], axis=1)
    grad_qkv_w = dot_tn(normed, grad_qkv)
    grad_normed = dot_nt(grad_qkv, qkv_w)
    grad_from_attn, grad_gain_attn = norm_back(grad_normed, unit_one, scale_one, gain_attn)
    grad_tokens = (grad_residual + grad_from_attn).astype(LOW)
    token_out = dot_tn(slot_hot, returned)
    layer_out = (residual + gate_value * token_out).astype(LOW)
    rel_rows = jnp.pad(
        grad_rel.reshape(groups, buckets_own * HEADS), ((0, 0), (0, share - buckets_own * HEADS))
    ).reshape(D, 1)
    summed = group_sum(
        jnp.concatenate(
            [
                grad_qkv_w.astype(LOW),
                grad_output_w.astype(LOW),
                grad_router_w.astype(LOW),
                grad_gain_attn.astype(LOW)[:, None],
                grad_gain_ffn.astype(LOW)[:, None],
                rel_rows.astype(LOW),
                jnp.zeros((D, small - experts - 3), LOW),
            ],
            axis=1,
        )
    )
    last = 3 * wide + D
    return (
        layer_out,
        grad_tokens,
        summed[:, :wide],
        summed[:, wide : 2 * wide],
        summed[:, 2 * wide : 3 * wide],
        summed[:, 3 * wide : last],
        summed[:, last : last + experts],
        summed[:, last + experts],
        summed[:, last + experts + 1],
        summed[: buckets_own * HEADS, last + experts + 2].reshape(buckets_own, HEADS),
        grad_first.astype(F32)[None],
        grad_second.astype(F32)[None],
    )


def dot_general_buckets(bucket_hot, diag):
    return lax.dot_general(
        bucket_hot.astype(F32), diag, (((1,), (1,)), ((), ())), precision=PRECISE
    )


def solution(mesh):
    placed = (
        P(("fsdp", "dp"), None),
        P(("fsdp", "dp"), None),
        P(("fsdp", "dp"), None),
        P(("fsdp", "dp"), None),
        P(),
        P("fsdp", None),
        P("fsdp", None),
        P("fsdp", None),
        P("fsdp", None),
        P("fsdp", None),
        P("fsdp"),
        P("fsdp"),
        P("fsdp", None),
        P("dp", None, "fsdp"),
        P("dp", "fsdp", None),
    )
    return jax.shard_map(
        local,
        mesh=mesh,
        in_specs=placed,
        out_specs=(
            P(("fsdp", "dp"), None),
            P(("fsdp", "dp"), None),
            P("fsdp", None),
            P("fsdp", None),
            P("fsdp", None),
            P("fsdp", None),
            P("fsdp", None),
            P("fsdp"),
            P("fsdp"),
            P("fsdp", None),
            P("dp", None, "fsdp"),
            P("dp", "fsdp", None),
        ),
        check_vma=False,
    )
```

time: 708 us -> 571 us (0.81)
  waiting for transfers between devices: 87.8 us -> 329 us
  local copies, waits for them, and re-layouts: 267 us -> 33 us
  blocking collectives: 131 us -> 0 us
  Pallas kernels: 0 us -> 44.7 us
  other arithmetic: 40.5 us -> 12.7 us
  matrix products: 135 us -> 111 us
    unnamed x79 -> x48, local copies, waits for them, and re-layouts: 121 us -> 7.7 us
    psum x1 -> x0, blocking collectives: 102 us -> none  [local(): lax.psum((shares[0], shares[1], shares[2], shares[3], shares[4], shares[5...]
    reduce_scatter x6 -> x3, waiting for transfers between devices: 0.05 us -> 89.5 us  [the longest x1 47.4 us: local(): lax.psum_scatter(first_term, 'fsdp', scatter_dimension=1, tiled=True)]
    psum x0 -> x1, waiting for transfers between devices: none -> 82.3 us  [group_sum(): return lax.psum(share, 'dp').astype(F32)]
    reshape x2 -> x5, local copies, waits for them, and re-layouts: 86.3 us -> 4.98 us  [the longest x2 4.03 us: swap(): rows.reshape(experts, -1, rows.shape[-1])]
    pallas_call x0 -> x2, Pallas kernels: none -> 44.7 us  [the longest x1 25 us: attend_back(): pl.pallas_call(attend_back_kernel, grid=(pairs,), in_specs=[pl.BlockSpec(...]
    all_gather x6 -> x3, waiting for transfers between devices: 0.09 us -> 39.7 us  [the longest x1 39.7 us: local(): packed = lax.all_gather(pack, 'fsdp', axis=0, tiled=True)]
    all_to_all x4, waiting for transfers between devices: 83.9 us -> 116 us  [swap(): lax.all_to_all(rows.reshape(experts, -1, rows.shape[-1]), 'dp', split_axi...]
  transfers between devices with their start and end apart: 17 -> 11, of which waited for: 4 -> 9; matrix products, arithmetic and copies ran while one was open for 61% -> 13% of each run, Pallas kernels for 0% -> 3%
where the time goes in v1:
time: 571 us; the launch traced here: 563 us
  waiting for transfers between devices  329 us (58%)
  matrix products  111 us (19%)
  Pallas kernels  44.7 us (8%)
  local copies, waits for them, and re-layouts  33 us (6%)
  starting transfers between devices  18.4 us (3%)
  between operations  14.9 us (3%)
  other arithmetic  12.7 us (2%)
    all_to_all x4, waiting for transfers between devices, swap(): lax.all_to_all(rows.reshape(experts, -1, rows.shape[-1]), 'dp', split_axi...  116 us
    psum x1, waiting for transfers between devices, group_sum(): return lax.psum(share, 'dp').astype(F32)  82.3 us
    reduce_scatter x1, waiting for transfers between devices, local(): lax.psum_scatter(first_term, 'fsdp', scatter_dimension=1, tiled=True)  47.4 us
    dot_general x9, matrix products, dot_nn(): return jnp.dot(a, b, preferred_element_type=F32)  45.2 us
    all_gather x1, waiting for transfers between devices, local(): packed = lax.all_gather(pack, 'fsdp', axis=0, tiled=True)  39.7 us
    dot_general x7, matrix products, dot_tn(): lax.dot_general(a, b, (((0,), (0,)), ((), ())), preferred_element_type=F32)  35.8 us
    reduce_scatter x1, waiting for transfers between devices, local(): lax.psum_scatter(second_term, 'fsdp', scatter_dimension=0, tiled=True)  25.9 us
    pallas_call x1, Pallas kernels, attend_back(): pl.pallas_call(attend_back_kernel, grid=(pairs,), in_specs=[pl.BlockSpec(...  25 us
  transfers between devices with their start and end apart: 11, of which 9 were waited for; matrix products, arithmetic and copies ran while one was open for 13% of the time, Pallas kernels for 3%

profile of v1, /device:TPU:0, one launch (start us, length us, event | category | flops | bytes accessed | tf_op | source)
XLA Modules:
  0.0 563.1 jit_solution(11615906231419735280)
XLA Ops:
  10.4 3.4 concatenate.13
  15.6 39.7 %all-gather.6.cloned.1.call-done = bf16[768,3200]{1,0:T(8,128)(2,1)} async-done(((bf16[192,3200]{1,0:T(8,128)(2,1)}), bf16[768,3200]{1,0:T(8,128)(2,1)}) %all-gather.6.cloned.1.call-update) | async-done | bytes 4915216 | tf_op jit(solution)/shard_map/all_gather | solution.py:228
  58.2 4.1 convolution_convert_fusion.3.q_ref.k_ref.v_ref
  62.3 19.6 %shard_map.238 = (bf16[512,768]{1,0:T(8,128)(2,1)S(1)}, bf16[12,512,512]{2,1,0:T(8,128)(2,1)S(1)}) custom-call(bf16[512,2304]{1,0:T(8,128)(2,1)S(1)} %convolution_convert_fusion.3.q_ref.k_ref.v_ref, bf16[512,2304]{1,0:T(8,128)(2,1)S(1)} %convolution_convert_fusion.3.q_ref.k_ref.v_ref, bf16[512,2304]{1,0:T(8,128)(2,1)S(1)} %convolution_convert_fusion.3.q_ref.k_ref.v_ref, ...), custom_call_target="tpu_custom_call" | custom-call | flops 805306368 | bytes 9437184 | tf_op jit(solution)/shard_map/pallas_call | solution.py:79
  90.1 5.5 all-to-all-start
  96.4 3.3 fusion.29
  102.3 30.9 %all-to-all-done = bf16[8,128,768]{2,1,0:T(8,128)(2,1)} async-done(((bf16[8,128,768]{2,1,0:T(8,128)(2,1)}), bf16[8,128,768]{2,1,0:T(8,128)(2,1)}, u32[]{:S(2)}, u32[]{:S(2)}) %all-to-all-start) | async-done | bytes 1572896 | tf_op jit(solution)/shard_map/all_to_all | solution.py:172
  133.2 4.6 all-to-all-start.1
  139.8 34.6 %all-to-all-done.1 = bf16[8,128,768]{1,2,0:T(8,128)(2,1)} async-done(((bf16[8,128,768]{1,2,0:T(8,128)(2,1)}), bf16[8,128,768]{1,2,0:T(8,128)(2,1)}, u32[]{:S(2)}, u32[]{:S(2)}) %all-to-all-start.1) | async-done | bytes 1572896 | tf_op jit(solution)/shard_map/all_to_all | solution.py:172
  174.4 10.6 %fusion.7 = f32[1024,3072]{1,0:T(8,128)} fusion(bf16[1,3072,768]{2,1,0:T(8,128)(2,1)} %all-gather.10.cloned.1.call-done, f32[1024]{0:T(1024)S(1)} %multiply_reduce_fusion.3, bf16[8,128,768]{1,2,0:T(8,128)(2,1)} %all-to-all-done.1), kind=kOutput, calls=%fused_computation.13 | convolution fusion | flops 4834197504 | bytes 18878464 | tf_op jit(solution)/shard_map/dot_general | solution.py:37
  185.0 18.9 %fusion.6 = (bf16[1024,3072]{1,0:T(8,128)(2,1)}, f32[1024,3072]{1,0:T(8,128)}) fusion(f32[1024,3072]{1,0:T(8,128)} %fusion.7, bf16[1024,768]{1,0:T(8,128)(2,1)} %bitcast.6, bf16[1,768,3072]{2,1,0:T(8,128)(2,1)} %all-gather.8.cloned.1.call-done), kind=kOutput, calls=%fused_computation.8 | convolution fusion | flops 4894752768 | bytes 37748736 | tf_op jit(solution)/shard_map/dot_general | solution.py:45
  204.0 10.4 %fusion.16 = (f32[1024]{0:T(1024)S(1)}, bf16[1024,768]{0,1:T(8,128)(2,1)}) fusion(bf16[1,3072,768]{2,1,0:T(8,128)(2,1)S(1)} %copy-done.15, f32[1024,3072]{1,0:T(8,128)} %get-tuple-element.119, bf16[8,128,768]{1,2,0:T(8,128)(2,1)} %all-to-all-done.1), kind=kOutput, calls=%fused_computation.25 | convolution fusion | flops 4864080896 | bytes 20451328 | tf_op jit(solution)/shard_map/dot_general | solution.py:45
  214.4 7.8 %fusion.11 = f32[1024,768]{1,0:T(8,128)S(1)} fusion(bf16[1024,3072]{1,0:T(8,128)(2,1)} %get-tuple-element.118, bf16[1,768,3072]{2,1,0:T(8,128)(2,1)S(1)} %copy-done.16), kind=kOutput, calls=%fused_computation.17 | convolution fusion | flops 4831838208 | bytes 14155776 | tf_op jit(solution)/shard_map/dot_general | solution.py:37
  222.2 3.7 add_convert_fusion
  225.9 4.3 all-to-all-start.2
  232.6 34.2 %all-to-all-done.2 = bf16[8,128,768]{2,1,0:T(8,128)(2,1)} async-done(((bf16[8,128,768]{2,1,0:T(8,128)(2,1)}), bf16[8,128,768]{2,1,0:T(8,128)(2,1)}, u32[]{:S(2)}, u32[]{:S(2)}) %all-to-all-start.2) | async-done | bytes 1572896 | tf_op jit(solution)/shard_map/all_to_all | solution.py:172
  266.8 3.4 multiply_reduce_fusion
  274.6 25.0 %shard_map.239 = (bf16[512,768]{1,0:T(8,128)(2,1)S(1)}, bf16[512,768]{1,0:T(8,128)(2,1)S(1)}, bf16[512,768]{1,0:T(8,128)(2,1)S(1)}, f32[12,1,1024]{2,1,0:T(1,128)S(1)}) custom-call(bf16[512,2304]{1,0:T(8,128)(2,1)S(1)} %convolution_convert_fusion.3.q_ref.k_ref.v_ref, bf16[512,2304]{1,0:T(8,128)(2,1)S(1)} %convolution_convert_fusion.3.q_ref.k_ref.v_ref, ...), custom_call_target="tpu_custom_call" | custom-call | flops 1610612736 | bytes 11796480 | tf_op jit(solution)/shard_map/pallas_call | solution.py:145
  300.8 3.9 convolution_convert_fusion.2
  304.7 3.3 fusion.39
  309.1 8.2 %concatenate.16 = bf16[768,3200]{1,0:T(8,128)(2,1)} concatenate(bf16[768,2304]{1,0:T(8,128)(2,1)} %convolution_convert_fusion.2, bf16[768,768]{1,0:T(8,128)(2,1)S(1)} %copy-done.7, bf16[768,8]{1,0:T(8,128)(2,1)S(1)} %copy.104, bf16[768,1]{1,0:T(8,128)(2,1)S(1)} %convert_element_type.210, bf16[768,1]{1,0:T(8,128)(2,1)S(1)} %convert_element_type.211, ...), dimensions={1} | concatenate | bytes 9830400 | tf_op jit(solution)/shard_map/concatenate | solution.py:315
  317.4 13.3 %convolution_convert_fusion = bf16[3072,768]{1,0:T(8,128)(2,1)} fusion(f32[1024]{0:T(1024)S(1)} %multiply_reduce_fusion.3, f32[1024,3072]{1,0:T(8,128)} %get-tuple-element.119, bf16[8,128,768]{1,2,0:T(8,128)(2,1)} %all-to-all-done.1), kind=kOutput, calls=%fused_computation.10 | convolution fusion | flops 4864868352 | bytes 18878464 | tf_op jit(solution)/shard_map/dot_general | solution.py:41
  330.8 9.3 %convolution_convert_fusion.1 = bf16[768,3072]{1,0:T(8,128)(2,1)} fusion(bf16[1024,768]{1,0:T(8,128)(2,1)} %bitcast.6, bf16[1024,3072]{1,0:T(8,128)(2,1)} %get-tuple-element.118), kind=kOutput, calls=%fused_computation.11 | convolution fusion | flops 4834197504 | bytes 12582912 | tf_op jit(solution)/shard_map/dot_general | solution.py:41
  342.9 3.8 all-to-all-start.3
  348.6 16.2 %reduce-scatter.4.cloned.1.call-done = bf16[192,3200]{1,0:T(8,128)(2,1)} async-done(((bf16[768,3200]{1,0:T(8,128)(2,1)}), bf16[192,3200]{1,0:T(8,128)(2,1)}) %reduce-scatter.4.cloned.1.call-update) | async-done | bytes 1228816 | tf_op jit(solution)/shard_map/reduce_scatter | solution.py:178
  364.9 3.0 fusion.38
  367.9 16.0 %all-to-all-done.3 = bf16[8,128,768]{1,2,0:T(8,128)(2,1)S(1)} async-done(((bf16[8,128,768]{1,2,0:T(8,128)(2,1)}), bf16[8,128,768]{1,2,0:T(8,128)(2,1)S(1)}, u32[]{:S(2)}, u32[]{:S(2)}) %all-to-all-start.3) | async-done | bytes 1572896 | tf_op jit(solution)/shard_map/all_to_all | solution.py:172
  385.5 3.9 add_convert_fusion.1
  389.3 25.9 %reduce-scatter.8.cloned.1.call-done = bf16[768,768]{1,0:T(8,128)(2,1)} async-done(((bf16[3072,768]{1,0:T(8,128)(2,1)}), bf16[768,768]{1,0:T(8,128)(2,1)}) %reduce-scatter.8.cloned.1.call-update) | async-done | bytes 1179664 | tf_op jit(solution)/shard_map/reduce_scatter | solution.py:290
  415.3 2.8 bitcast_convert_fusion
  418.1 47.4 %reduce-scatter.6.cloned.1.call-done = bf16[768,768]{1,0:T(8,128)(2,1)} async-done(((bf16[768,3072]{1,0:T(8,128)(2,1)}), bf16[768,768]{1,0:T(8,128)(2,1)}) %reduce-scatter.6.cloned.1.call-update) | async-done | bytes 1179664 | tf_op jit(solution)/shard_map/reduce_scatter | solution.py:289
  468.4 82.3 %all-reduce.4.cloned.1.call-done = bf16[192,3200]{1,0:T(8,128)(2,1)} async-done(((bf16[192,3200]{1,0:T(8,128)(2,1)}), bf16[192,3200]{1,0:T(8,128)(2,1)}) %all-reduce.4.cloned.1.call-update) | async-done | bytes 1228816 | tf_op jit(solution)/shard_map/psum | solution.py:179
  (123 shorter events, 44.9 us)
Async XLA Ops:
  7.2 48.1 %all-gather.6.cloned.1.call-start = ((), (), s32[]{:S(2)}) async-start(), calls=%async_computation.7 | async-start | bytes 6144000 | tf_op jit(solution)/shard_map/all_gather | solution.py:228
  10.4 4.2 copy-start.17
  10.4 4.7 copy-start.14
  10.4 4.7 copy-start.13
  10.4 4.9 copy-start.8
  13.8 160.5 %all-gather.10.cloned.1.call-start = ((), (), s32[]{:S(2)}) async-start(), calls=%async_computation.13 | async-start | bytes 5898240 | tf_op jit(solution)/shard_map/all_gather | solution.py:241
  62.3 22.2 %copy-start.9 = (bf16[512,768]{1,0:T(8,128)(2,1)S(1)}, bf16[512,768]{1,0:T(8,128)(2,1)}, u32[]{:S(2)}) copy-start(bf16[512,768]{1,0:T(8,128)(2,1)} %param.15) | copy-start | bytes 2359300
  81.9 2.6 copy-start
  86.7 1.1 copy-start.4
  90.1 43.0 %all-to-all-start = ((bf16[8,128,768]{2,1,0:T(8,128)(2,1)}), bf16[8,128,768]{2,1,0:T(8,128)(2,1)}, u32[]{:S(2)}, u32[]{:S(2)}) async-start(bf16[8,128,768]{2,1,0:T(8,128)(2,1)} %bitcast.76), calls=%async_computation | async-start | bytes 3145728 | tf_op jit(solution)/shard_map/all_to_all | solution.py:172
  95.7 89.3 %all-gather.8.cloned.1.call-start = ((), (), s32[]{:S(2)}) async-start(), calls=%async_computation.12 | async-start | bytes 5898240 | tf_op jit(solution)/shard_map/all_gather | solution.py:240
  133.2 41.2 %all-to-all-start.1 = ((bf16[8,128,768]{1,2,0:T(8,128)(2,1)}), bf16[8,128,768]{1,2,0:T(8,128)(2,1)}, u32[]{:S(2)}, u32[]{:S(2)}) async-start(bf16[8,128,768]{1,2,0:T(8,128)(2,1)} %copy.98), calls=%async_computation.1 | async-start | bytes 3145728 | tf_op jit(solution)/shard_map/all_to_all | solution.py:172
  185.0 19.0 %copy-start.15 = (bf16[1,3072,768]{2,1,0:T(8,128)(2,1)S(1)}, bf16[1,3072,768]{2,1,0:T(8,128)(2,1)}, u32[]{:S(2)}) copy-start(bf16[1,3072,768]{2,1,0:T(8,128)(2,1)} %all-gather.10.cloned.1.call-done) | copy-start | bytes 14155780
  204.0 10.4 %copy-start.16 = (bf16[1,768,3072]{2,1,0:T(8,128)(2,1)S(1)}, bf16[1,768,3072]{2,1,0:T(8,128)(2,1)}, u32[]{:S(2)}) copy-start(bf16[1,768,3072]{2,1,0:T(8,128)(2,1)} %all-gather.8.cloned.1.call-done) | copy-start | bytes 14155780
  225.9 40.9 %all-to-all-start.2 = ((bf16[8,128,768]{2,1,0:T(8,128)(2,1)}), bf16[8,128,768]{2,1,0:T(8,128)(2,1)}, u32[]{:S(2)}, u32[]{:S(2)}) async-start(bf16[8,128,768]{2,1,0:T(8,128)(2,1)} %bitcast.75), calls=%async_computation.2 | async-start | bytes 3145728 | tf_op jit(solution)/shard_map/all_to_all | solution.py:172
  230.2 134.6 %reduce-scatter.4.cloned.1.call-start = ((), (), s32[]{:S(2)}) async-start(), calls=%async_computation.8 | async-start | bytes 6144000 | tf_op jit(solution)/shard_map/reduce_scatter | solution.py:178
  266.8 3.4 copy-start.5
  266.8 3.4 copy-start.12
  266.8 7.8 %slice-start = ((s8[6291456]{0:T(1024)(128)(4,1)}), s8[4194304]{0:T(1024)(128)(4,1)S(1)}, s32[]{:S(2)}) async-start(s8[6291456]{0:T(1024)(128)(4,1)} %bitcast.71), calls=%async_computation.14 | async-start | bytes 8388608
  270.2 4.4 slice-start.1
  270.7 3.9 copy-start.1
  299.7 5.0 slice-start.2
  300.8 3.9 slice-start.3
  304.7 4.4 copy-start.7
  317.4 97.9 %reduce-scatter.8.cloned.1.call-start = ((), (), s32[]{:S(2)}) async-start(), calls=%async_computation.11 | async-start | bytes 5898240 | tf_op jit(solution)/shard_map/reduce_scatter | solution.py:290
  330.7 134.8 %reduce-scatter.6.cloned.1.call-start = ((), (), s32[]{:S(2)}) async-start(), calls=%async_computation.10 | async-start | bytes 5898240 | tf_op jit(solution)/shard_map/reduce_scatter | solution.py:289
  340.1 1.4 copy-start.11
  342.9 21.9 %copy-start.2 = (f32[512,768]{1,0:T(8,128)S(1)}, f32[512,768]{1,0:T(8,128)}, u32[]{:S(2)}) copy-start(f32[512,768]{1,0:T(8,128)} %copy-done.1) | copy-start | bytes 4718596
  342.9 40.9 %all-to-all-start.3 = ((bf16[8,128,768]{1,2,0:T(8,128)(2,1)}), bf16[8,128,768]{1,2,0:T(8,128)(2,1)S(1)}, u32[]{:S(2)}, u32[]{:S(2)}) async-start(bf16[8,128,768]{1,2,0:T(8,128)(2,1)} %copy_bitcast_fusion), calls=%async_computation.3 | async-start | bytes 3145728 | tf_op jit(solution)/shard_map/all_to_all | solution.py:172
  346.7 204.0 %all-reduce.4.cloned.1.call-start = ((), (), s32[]{:S(2)}) async-start(), calls=%async_computation.9 | async-start | bytes 2457600 | tf_op jit(solution)/shard_map/psum | solution.py:179
  367.9 17.6 %copy-start.6 = (f32[512,768]{1,0:T(8,128)S(1)}, f32[512,768]{1,0:T(8,128)}, u32[]{:S(2)}) copy-start(f32[512,768]{1,0:T(8,128)} %copy-done.4) | copy-start | bytes 4718596
  550.7 3.2 copy-start.3
  (1 other events, 1.1 us)
Sparse Core Ops, SparseCore 0:
  14.0 41.2 all-gather.5
  56.8 37.4 all-gather.9
  98.0 37.9 all-gather.7
  317.5 47.3 reduce-scatter.3
  367.4 47.8 reduce-scatter.7
  417.6 47.8 reduce-scatter.5
  469.5 81.1 all-reduce.3
